TPU v7x, 256 devices: a whole 4x4x8 slice. The times are simulated.
256 devices in a mesh: enc: 32 (over y, z), dec: 4 (over x), mdl: 2 (over core).
Axes of the slice: x: 4, y: 4, z: 8, core: 2. Of those that a mesh axis runs over, the one named last changes fastest.
Arguments:
- passages: bfloat16 [384, 256, 4096], P(('enc', 'dec')), may hold values from -6 to 6
- norm_gain: bfloat16 [4096], replicated, may hold values from 0.099609375 to 1.8984375
- w_key: bfloat16 [4096, 2048], P(('enc', 'dec'), 'mdl'), may hold values from -0.09375 to 0.09375
- w_value: bfloat16 [4096, 2048], P(('enc', 'dec'), 'mdl'), may hold values from -0.375 to 0.375
- queries: bfloat16 [64, 64, 2048], P('enc', None, 'mdl'), may hold values from -18 to 18
- lengths: int32 [384], P(('enc', 'dec')), may hold values from 1 to 256
- passage_question: int32 [384], P(('enc', 'dec')), may hold values from 0 to 63, as said below
Outputs:
- context: bfloat16 [64, 64, 2048], P('enc', None, 'mdl')
Inputs may be any that keep to these rules, and one draw needn't show every extreme that they name: Passage p serves a question of its own group: p // 12 * 2 <= passage_question[p] < (p // 12 + 1) * 2, and every question has at least one passage.
All inputs are finite; a program needn't handle non-finite values.
Results may differ from a plain program's by a relative error of at most 0.009.
The roundings to bfloat16 on the way count: a program that leaves them out, or rounds other values in their place, can miss the bound.
Values may be sent and summed in bfloat16 or wider, within the bound.
No kernel may reach another device: no remote copies, remote signals or barrier semaphores. Data moves between devices by JAX's collectives and lax.ppermute only.
A program may use at most 128 MiB of HBM per device.

v0:
```python
import jax
import jax.numpy as jnp
from jax import lax
from jax.sharding import PartitionSpec as P

HD = 64


def joined(value, axis, join):
    pieces = jax.tree.map(lambda part: lax.all_gather(part, axis), value)
    head = jax.tree.map(lambda part: part[0], pieces)
    tail = jax.tree.map(lambda part: part[1:], pieces)
    subtotal, _ = lax.scan(lambda subtotal, slab: (join(subtotal, slab), None), head, tail)
    return subtotal


def combine_partials(earlier, later):
    joint_max = jnp.maximum(earlier[0], later[0])
    first_scale = jnp.exp(earlier[0] - joint_max)
    second_scale = jnp.exp(later[0] - joint_max)
    totals = earlier[1] * first_scale + later[1] * second_scale
    numerators = earlier[2] * first_scale[..., None] + later[2] * second_scale[..., None]
    return (joint_max, totals, numerators)


def body(passages, norm_gain, w_key, w_value, queries, lengths, passage_question):
    pass_local, slot_count, width = passages.shape
    states = passages.reshape(pass_local * slot_count, width).astype(jnp.float32)
    scale = lax.rsqrt(jnp.mean(states * states, axis=1, keepdims=True) + 1e-06)
    normed = (states * scale * norm_gain.astype(jnp.float32)).astype(jnp.bfloat16)
    full_key = lax.all_gather(w_key, ("enc", "dec"), axis=0, tiled=True)
    full_value = lax.all_gather(w_value, ("enc", "dec"), axis=0, tiled=True)
    columns = full_key.shape[1]
    key_rows = jnp.dot(normed, full_key, preferred_element_type=jnp.float32).astype(jnp.bfloat16)
    value_rows = jnp.dot(normed, full_value, preferred_element_type=jnp.float32).astype(
        jnp.bfloat16
    )
    heads_local = columns // HD
    q_local, answer_len = (queries.shape[0], queries.shape[1])
    row_count = q_local * answer_len
    key_count = pass_local * slot_count
    query_heads = queries.reshape(row_count, heads_local, HD)
    key_heads = key_rows.reshape(key_count, heads_local, HD)
    value_heads = value_rows.reshape(key_count, heads_local, HD)
    scores = jnp.einsum("rhc,khc->hrk", query_heads, key_heads, preferred_element_type=jnp.float32)
    group_first = lax.axis_index("enc") * q_local
    row_question = group_first + jnp.arange(row_count, dtype=jnp.int32) // answer_len
    key_question = jnp.repeat(passage_question, slot_count)
    slot_index = jnp.arange(key_count, dtype=jnp.int32) % slot_count
    key_live = slot_index < jnp.repeat(lengths, slot_count)
    allowed = (row_question[:, None] == key_question[None, :]) & key_live[None, :]
    masked = jnp.where(allowed[None], scores, -1e30)
    local_max = jnp.max(masked, axis=2)
    weights = jnp.where(allowed[None], jnp.exp(masked - local_max[..., None]), 0.0)
    local_total = jnp.sum(weights, axis=2)
    local_numer = jnp.einsum(
        "hrk,khc->hrc",
        weights.astype(jnp.bfloat16),
        value_heads,
        preferred_element_type=jnp.float32,
    )
    joint_max, totals, numerators = joined(
        (local_max, local_total, local_numer), "dec", combine_partials
    )
    result = numerators / totals[..., None]
    return (
        jnp.transpose(result, (1, 0, 2))
        .reshape(q_local, answer_len, heads_local * HD)
        .astype(jnp.bfloat16)
    )


def solution(mesh):
    return jax.shard_map(
        body,
        mesh=mesh,
        in_specs=(
            P(("enc", "dec"), None, None),
            P(),
            P(("enc", "dec"), "mdl"),
            P(("enc", "dec"), "mdl"),
            P("enc", None, "mdl"),
            P(("enc", "dec")),
            P(("enc", "dec")),
        ),
        out_specs=P("enc", None, "mdl"),
        check_vma=False,
    )
```

profile of v0, /device:TPU:1, one launch (start us, length us, event | category | flops | bytes accessed | tf_op | source)
XLA Modules:
  0.0 334.7 jit_solution(2678174987800341566)
XLA Ops:
  6.5 0.0 copy-start.2
  6.5 0.0 all-gather.7.cloned.1.call-start
  6.5 0.7 all-gather.7.cloned.1.call-update
  7.3 0.0 all-gather.9.cloned.1.call-start
  7.3 0.7 all-gather.9.cloned.1.call-update
  8.0 0.0 all-gather.11.cloned.1.call-start
  8.1 0.7 broadcast_in_dim.35
  8.8 0.7 broadcast_in_dim.34
  9.5 0.7 convert_element_type.36
  10.2 4.1 %multiply_reduce_fusion = f32[3,256]{1,0:T(4,128)S(1)} fusion(bf16[3,256,4096]{2,1,0:T(8,128)(2,1)} %param.9), kind=kLoop, calls=%fused_computation.12 | loop fusion | flops 9436416 | bytes 6294528 | tf_op jit(solution)/shard_map/reduce_sum | solution.py:29
  14.3 0.0 copy-done.2
  14.3 0.3 reshape.115
  14.7 0.3 compare_and_fusion
  15.0 8.2 %fusion.4 = bf16[768,4096]{1,0:T(8,128)(2,1)} fusion(f32[4096]{0:T(1024)S(1)} %convert_element_type.36, f32[768]{0:T(1024)S(1)} %rsqrt.12, bf16[3,256,4096]{2,1,0:T(8,128)(2,1)} %param.9), kind=kLoop, calls=%fused_computation.11 | loop fusion | flops 12582912 | bytes 12602368 | tf_op jit(solution)/shard_map/convert_element_type | solution.py:30
  23.2 112.8 %all-gather.7.cloned.1.call-done = bf16[4096,1024]{1,0:T(8,128)(2,1)} async-done(((bf16[32,1024]{1,0:T(8,128)(2,1)}), bf16[4096,1024]{1,0:T(8,128)(2,1)}) %all-gather.7.cloned.1.call-update) | async-done | bytes 8388624 | tf_op jit(solution)/shard_map/all_gather | solution.py:31
  135.9 12.1 %convolution_convert_fusion.1 = bf16[768,1024]{1,0:T(8,128)(2,1)} fusion(bf16[768,4096]{1,0:T(8,128)(2,1)} %fusion.4, bf16[4096,1024]{1,0:T(8,128)(2,1)} %all-gather.7.cloned.1.call-done), kind=kOutput, calls=%fused_computation.21 | convolution fusion | flops 6443237376 | bytes 16252928 | tf_op jit(solution)/shard_map/dot_general | solution.py:34
  148.0 1.7 copy.22
  149.7 110.6 %all-gather.9.cloned.1.call-done = bf16[4096,1024]{1,0:T(8,128)(2,1)} async-done(((bf16[32,1024]{1,0:T(8,128)(2,1)}), bf16[4096,1024]{1,0:T(8,128)(2,1)}) %all-gather.9.cloned.1.call-update) | async-done | bytes 8388624 | tf_op jit(solution)/shard_map/all_gather | solution.py:32
  260.3 12.0 %convolution_convert_fusion = bf16[768,1024]{1,0:T(8,128)(2,1)} fusion(bf16[768,4096]{1,0:T(8,128)(2,1)} %fusion.4, bf16[4096,1024]{1,0:T(8,128)(2,1)} %all-gather.9.cloned.1.call-done), kind=kOutput, calls=%fused_computation.20 | convolution fusion | flops 6443237376 | bytes 16252928 | tf_op jit(solution)/shard_map/dot_general | solution.py:35
  272.3 2.6 copy.24
  274.9 0.0 copy-start.1
  274.9 1.3 fusion.5
  276.3 0.0 copy-start
  276.3 2.7 copy-done
  278.9 0.0 copy-done.1
  278.9 2.6 fusion.8
  281.5 0.0 all-gather.11.cloned.1.call-update
  281.5 4.1 %fusion.7 = f32[16,128]{1,0:T(8,128)S(1)} fusion(f32[16,768,128]{2,1,0:T(8,128)} %copy-done, f32[16,128]{1,0:T(8,128)S(1)} %get-tuple-element.84, pred[128,768]{0,1:T(8,128)(4,1)S(1)} %compare_and_fusion), kind=kLoop, calls=%fused_computation.17 | loop fusion | flops 6289408 | bytes 6406144 | tf_op jit(solution)/shard_map/reduce_sum | solution.py:55
  285.6 9.3 %all-gather.1 = f32[64,128]{1,0:T(8,128)S(1)} all-gather(f32[16,128]{1,0:T(8,128)S(1)} %fusion.7), channel_id=3, replica_groups=mesh['enc'=32,'dec'=4,'mdl'=2] {'dec'}, dimensions={0}, use_global_device_ids=true | all-gather | bytes 40960 | tf_op jit(solution)/shard_map/all_gather | solution.py:10
  294.9 10.1 %all-gather = f32[64,128]{1,0:T(8,128)S(1)} all-gather(f32[16,128]{1,0:T(8,128)S(1)} %get-tuple-element.84), channel_id=2, replica_groups=mesh['enc'=32,'dec'=4,'mdl'=2] {'dec'}, dimensions={0}, use_global_device_ids=true | all-gather | bytes 40960 | tf_op jit(solution)/shard_map/all_gather | solution.py:10
  305.1 9.9 %all-gather.11.cloned.1.call-done = f32[64,128,64]{1,2,0:T(8,128)} async-done(((f32[16,128,64]{1,2,0:T(8,128)}), f32[64,128,64]{1,2,0:T(8,128)}) %all-gather.11.cloned.1.call-update) | async-done | bytes 2097168 | tf_op jit(solution)/shard_map/all_gather | solution.py:10
  315.0 1.1 slice.32
  316.1 0.3 copy.26
  316.4 2.7 slice.35
  319.1 7.3 %while.14 = (s32[]{:T(128)}, f32[16,128]{1,0:T(8,128)S(1)}, f32[16,128]{1,0:T(8,128)S(1)}, f32[16,128,64]{2,1,0:T(8,128)S(1)}, f32[3,16,128]{2,1,0:T(8,128)S(1)}...) while((s32[]{:T(128)}, f32[16,128]{1,0:T(8,128)S(1)}, f32[16,128]{1,0:T(8,128)S(1)}, ...), condition=%wide.region_4.5_spmd, body=%wide.region_3.4_spmd.sunk | while | flops 405506 | bytes 3752029 | solution.py:13
  319.2 1.1 constant_dynamic-slice_fusion.2
  320.2 0.3 copy.36
  320.6 1.0 fusion.31
  321.6 1.1 constant_dynamic-slice_fusion.2
  322.7 0.3 copy.36
  323.0 1.0 fusion.31
  324.0 1.1 constant_dynamic-slice_fusion.2
  325.1 0.3 copy.36
  325.5 1.0 fusion.31
  326.5 0.3 fusion.13
  326.8 0.3 copy.28
  327.2 1.1 convert_element_type.43
  (13 shorter events, 0.1 us)
Async XLA Ops:
  6.5 7.8 %copy-start.2 = (bf16[2,64,1024]{2,1,0:T(8,128)(2,1)S(1)}, bf16[2,64,1024]{2,1,0:T(8,128)(2,1)}, u32[]{:S(2)}) copy-start(bf16[2,64,1024]{2,1,0:T(8,128)(2,1)} %param.13) | copy-start | bytes 786436
  6.5 129.4 %all-gather.7.cloned.1.call-start = ((), (), s32[]{:S(2)}) async-start(), calls=%async_computation | async-start | bytes 8454144 | tf_op jit(solution)/shard_map/all_gather | solution.py:31
  7.3 253.0 %all-gather.9.cloned.1.call-start = ((), (), s32[]{:S(2)}) async-start(), calls=%async_computation.1 | async-start | bytes 8454144 | tf_op jit(solution)/shard_map/all_gather | solution.py:32
  8.0 307.0 %all-gather.11.cloned.1.call-start = ((), (), s32[]{:S(2)}) async-start(), calls=%async_computation.2 | async-start | bytes 2621440 | tf_op jit(solution)/shard_map/all_gather | solution.py:10
  274.9 4.0 %copy-start.1 = (bf16[768,1024]{0,1:T(8,128)(2,1)S(1)}, bf16[768,1024]{0,1:T(8,128)(2,1)}, u32[]{:S(2)}) copy-start(bf16[768,1024]{0,1:T(8,128)(2,1)} %copy.24) | copy-start | bytes 4718596
  276.3 2.7 copy-start
Sparse Core Ops, SparseCore 0:
  11.0 124.9 all-gather.6
  139.5 120.6 all-gather.8
  281.6 33.2 all-gather.10
where the time goes:
time: 335 us
  waiting for transfers between devices  235 us (70%)
  matrix products  28 us (8%)
  other arithmetic  20.6 us (6%)
  blocking collectives  19.5 us (6%)
  local copies, waits for them, and re-layouts  18.6 us (6%)
  between operations  13.2 us (4%)
    all_gather x1, waiting for transfers between devices, body(): full_key = lax.all_gather(w_key, ('enc', 'dec'), axis=0, tiled=True)  113 us
    all_gather x1, waiting for transfers between devices, body(): full_value = lax.all_gather(w_value, ('enc', 'dec'), axis=0, tiled=True)  111 us
    all_gather x2, blocking collectives, joined(): pieces = jax.tree.map(lambda part: lax.all_gather(part, axis), value)  19.5 us
    dot_general x1, matrix products, body(): jnp.dot(normed, full_key, preferred_element_type=jnp.float32)  12.1 us
    dot_general x1, matrix products, body(): jnp.dot(normed, full_value, preferred_element_type=jnp.float32)  12 us
    all_gather x1, waiting for transfers between devices, joined(): pieces = jax.tree.map(lambda part: lax.all_gather(part, axis), value)  9.9 us
    convert_element_type x1, other arithmetic, body(): (states * scale * norm_gain.astype(jnp.float32)).astype(jnp.bfloat16)  8.17 us
  transfers between devices with their start and end apart: 3, of which 3 were waited for; matrix products, arithmetic and copies ran while one was open for 10% of the time, Pallas kernels for 0%

commit v1 on v0

v1 whole, which is shorter than its diff:
```python
import functools

import jax
import jax.numpy as jnp
from jax import lax
from jax.experimental import pallas as pl
from jax.experimental.pallas import tpu as pltpu
from jax.sharding import PartitionSpec as P

HD = 64
NY, NZ, NX, NC = 4, 8, 4, 2
DY = (0, -1, 1, 2)
DZ = (0, -1, -2, -3, 1, 2, 3, 4)
VMEM_LIMIT = 56 * 1024 * 1024
NEG = -1e30
TILE = 384
UNIT = 128


def shift_z(value, step):
    pairs = [(y * NZ + z, y * NZ + (z + step) % NZ) for y in range(NY) for z in range(NZ)]
    return lax.ppermute(value, "enc", pairs)


def shift_y(value, step):
    pairs = [(y * NZ + z, (y + step) % NY * NZ + z) for y in range(NY) for z in range(NZ)]
    return lax.ppermute(value, "enc", pairs)


def shift_x(value, step):
    return lax.ppermute(value, "dec", [(x, (x + step) % NX) for x in range(NX)])


def split_x(value):
    pairs = [
        (x * NC + c, (x + (1 if c == 0 else -1)) % NX * NC + c) for x in range(NX) for c in range(NC)
    ]
    return lax.ppermute(value, ("dec", "mdl"), pairs)


def other_core(value):
    return lax.ppermute(value, "mdl", [(0, 1), (1, 0)])


def norm_kernel(order_ref, x_ref, gain_ref, o_ref):
    states = x_ref[...].astype(jnp.float32)
    width = states.shape[1]
    scale = lax.rsqrt(jnp.sum(states * states, axis=1, keepdims=True) * (1.0 / width) + 1e-06)
    for k in range(width // 128):
        start = pl.multiple_of(order_ref[k] * 128, 128)
        part = x_ref[:, pl.ds(start, 128)].astype(jnp.float32)
        gain = gain_ref[:, pl.ds(start, 128)].astype(jnp.float32)
        o_ref[:, k * 128 : (k + 1) * 128] = (part * scale * gain).astype(jnp.bfloat16)


def normalise(order, states, gain):
    rows, width = states.shape
    return pl.pallas_call(
        norm_kernel,
        out_shape=jax.ShapeDtypeStruct((rows, width), jnp.bfloat16),
        grid_spec=pltpu.PrefetchScalarGridSpec(
            num_scalar_prefetch=1,
            grid=(rows // UNIT,),
            in_specs=[
                pl.BlockSpec((UNIT, width), lambda i, order: (i, 0)),
                pl.BlockSpec((1, width), lambda i, order: (0, 0)),
            ],
            out_specs=pl.BlockSpec((UNIT, width), lambda i, order: (i, 0)),
        ),
        compiler_params=pltpu.CompilerParams(vmem_limit_bytes=VMEM_LIMIT),
        cost_estimate=pl.CostEstimate(
            flops=6 * rows * width, bytes_accessed=4 * rows * width, transcendentals=rows
        ),
    )(order, states, gain)


def value_columns(x, j):
    return jnp.concatenate(
        [x[:, i * 1024 + j * 128 : i * 1024 + (j + 1) * 128] for i in range(NY)], axis=1
    )


def project_kernel(own_ref, near_ref, far_ref, *refs):
    key_refs, value_refs = refs[:3], refs[3:10]
    key_out, value_out, rest_out = refs[10:]
    step = pl.program_id(0)

    def run(x_ref):
        total = None
        for i, w_ref in enumerate(key_refs):
            part = jnp.dot(
                x_ref[:, i * 1024 : (i + 1) * 1024], w_ref[...], preferred_element_type=jnp.float32
            )
            total = part if total is None else total + part
        key_out[...] = total
        total = None
        for j, w_ref in enumerate(value_refs):
            part = jnp.dot(
                value_columns(x_ref, j), w_ref[...], preferred_element_type=jnp.float32
            )
            total = part if total is None else total + part
        value_out[...] = total
        rest_out[:, :1024] = x_ref[:, 3072:4096]
        rest_out[:, 1024:] = value_columns(x_ref, 7)

    pl.when(step < 2)(lambda: run(own_ref))
    pl.when(step == 2)(lambda: run(near_ref))
    pl.when(step == 3)(lambda: run(far_ref))


def project(own, near, far, key_parts, value_parts):
    rows = own.shape[0] + near.shape[0] + far.shape[0]
    width, cols = own.shape[1], key_parts[0].shape[1]
    steps = rows // TILE
    whole = lambda a: pl.BlockSpec(a.shape, lambda i: (0, 0))
    return pl.pallas_call(
        project_kernel,
        out_shape=(
            jax.ShapeDtypeStruct((rows, cols), jnp.float32),
            jax.ShapeDtypeStruct((rows, cols), jnp.float32),
            jax.ShapeDtypeStruct((rows, 1536), jnp.bfloat16),
        ),
        grid=(steps,),
        in_specs=[
            pl.BlockSpec((TILE, width), lambda i: (jnp.minimum(i, 1), 0)),
            whole(near),
            whole(far),
        ]
        + [whole(a) for a in key_parts]
        + [whole(a) for a in value_parts],
        out_specs=(
            pl.BlockSpec((TILE, cols), lambda i: (i, 0)),
            pl.BlockSpec((TILE, cols), lambda i: (i, 0)),
            pl.BlockSpec((TILE, 1536), lambda i: (i, 0)),
        ),
        compiler_params=pltpu.CompilerParams(vmem_limit_bytes=VMEM_LIMIT),
        cost_estimate=pl.CostEstimate(
            flops=2 * rows * cols * (3072 + 3584),
            bytes_accessed=rows * width * 2 + 6656 * cols * 2 + rows * cols * 8,
            transcendentals=0,
        ),
    )(own, near, far, *key_parts, *value_parts)


def split3(x):
    high = x.astype(jnp.bfloat16)
    rest = x - high.astype(jnp.float32)
    mid = rest.astype(jnp.bfloat16)
    low = (rest - mid.astype(jnp.float32)).astype(jnp.bfloat16)
    return [high, mid, low]


def attend_kernel(
    owner_ref, live_ref, key_acc, value_acc, rest_ref, wk0, wk1, wv0, wv1, q_ref, o_ref, num, top, tot
):
    step = pl.program_id(0)

    @pl.when(step == 0)
    def _():
        num[...] = jnp.zeros_like(num)
        tot[...] = jnp.zeros_like(tot)
        top[...] = jnp.full_like(top, NEG)

    def dot(a, b):
        return jnp.dot(a, b, preferred_element_type=jnp.float32)

    keys = key_acc[...] + dot(rest_ref[:, :512], wk0[...]) + dot(rest_ref[:, 512:1024], wk1[...])
    keys = keys.astype(jnp.bfloat16)
    values = (
        value_acc[...] + dot(rest_ref[:, 1024:1280], wv0[...]) + dot(rest_ref[:, 1280:], wv1[...])
    )
    values = values.astype(jnp.bfloat16)
    slot = lax.broadcasted_iota(jnp.int32, (UNIT, 256), 0)
    for u in range(TILE // UNIT):
        unit = step * (TILE // UNIT) + u
        valid = slot < live_ref[unit]
        for g in range(2):
            at = owner_ref[unit] * 2 + g
            part = (slice(u * UNIT, (u + 1) * UNIT), slice(g * 256, (g + 1) * 256))
            scores = jnp.where(valid, dot(keys[part], q_ref[at]), NEG)
            old = top[at, 0:1, :]
            new = jnp.maximum(old, jnp.max(scores, axis=0, keepdims=True))
            fade = jnp.exp(old - new)
            weights = jnp.where(valid, jnp.exp(scores - new), 0.0)
            top[at, 0:1, :] = new
            tot[at, 0:1, :] = tot[at, 0:1, :] * fade + jnp.sum(weights, axis=0, keepdims=True)
            added = lax.dot_general(
                values[part],
                weights.astype(jnp.bfloat16),
                (((0,), (0,)), ((), ())),
                preferred_element_type=jnp.float32,
            )
            num[at] = num[at] * fade + added

    @pl.when(step == pl.num_programs(0) - 1)
    def _():
        for head in range(8):
            g, a = head // 4, head % 4 * HD
            join = lambda ref, r0, r1: jnp.concatenate(
                [ref[q * 2 + g, r0:r1, a : a + HD] for q in range(2)], axis=1
            )
            o_ref[head, :HD, :] = join(num, a, a + HD).astype(jnp.bfloat16)
            lines = split3(join(top, 0, 1)) + split3(join(tot, 0, 1))
            lines.append(jnp.zeros((10, 128), jnp.bfloat16))
            o_ref[head, HD:, :] = jnp.concatenate(lines, axis=0)


def attend(owner, live, key_acc, value_acc, rest, key_last, value_last, query_blocks):
    rows, cols = key_acc.shape
    whole = lambda a: pl.BlockSpec(a.shape, lambda i, *_: (0,) * a.ndim)
    tiled = lambda a: pl.BlockSpec((TILE, a.shape[1]), lambda i, *_: (i, 0))
    ends = list(key_last) + list(value_last)
    return pl.pallas_call(
        attend_kernel,
        out_shape=jax.ShapeDtypeStruct((8, 80, 128), jnp.bfloat16),
        grid_spec=pltpu.PrefetchScalarGridSpec(
            num_scalar_prefetch=2,
            grid=(rows // TILE,),
            in_specs=[tiled(key_acc), tiled(value_acc), tiled(rest)]
            + [whole(a) for a in ends]
            + [whole(query_blocks)],
            out_specs=pl.BlockSpec((8, 80, 128), lambda i, *_: (0, 0, 0)),
            scratch_shapes=[
                pltpu.VMEM((4, 256, 256), jnp.float32),
                pltpu.VMEM((4, 8, 256), jnp.float32),
                pltpu.VMEM((4, 8, 256), jnp.float32),
            ],
        ),
        compiler_params=pltpu.CompilerParams(vmem_limit_bytes=VMEM_LIMIT),
        cost_estimate=pl.CostEstimate(
            flops=2 * rows * cols * (1536 + 1024),
            bytes_accessed=rows * cols * 8 + rows * 1536 * 2 + 1536 * cols * 2,
            transcendentals=rows * 512,
        ),
    )(owner, live, key_acc, value_acc, rest, *ends, query_blocks)


def combine_kernel(colour_ref, own, opposite, left, right, o_ref):
    def exact(ref, head, row):
        part = lambda r: ref[head, r : r + 1, :].astype(jnp.float32)
        return part(row) + part(row + 1) + part(row + 2)

    def head_result(a, b, head):
        top_a, top_b = exact(a, head, HD), exact(b, head, HD)
        top = jnp.maximum(top_a, top_b)
        fade_a, fade_b = jnp.exp(top_a - top), jnp.exp(top_b - top)
        total = exact(a, head, HD + 3) * fade_a + exact(b, head, HD + 3) * fade_b
        sums = a[head, :HD, :].astype(jnp.float32) * fade_a
        sums = sums + b[head, :HD, :].astype(jnp.float32) * fade_b
        return sums / total

    for side, (a, b) in enumerate(((own, opposite), (left, right))):
        colour = colour_ref[0] if side == 0 else 1 - colour_ref[0]
        for pair in range(4):
            block = jnp.concatenate(
                [head_result(a, b, 2 * pair), head_result(a, b, 2 * pair + 1)], axis=0
            )
            start = pl.multiple_of(colour * 512 + pair * 128, 128)
            o_ref[:, pl.ds(start, 128)] = block.T.astype(jnp.bfloat16)


def combine(colour, own, opposite, left, right):
    return pl.pallas_call(
        combine_kernel,
        out_shape=jax.ShapeDtypeStruct((128, 1024), jnp.bfloat16),
        in_specs=[pl.BlockSpec(memory_space=pltpu.SMEM)]
        + [pl.BlockSpec(memory_space=pltpu.VMEM)] * 4,
        out_specs=pl.BlockSpec(memory_space=pltpu.VMEM),
        compiler_params=pltpu.CompilerParams(vmem_limit_bytes=VMEM_LIMIT),
        cost_estimate=pl.CostEstimate(flops=1 << 20, bytes_accessed=1 << 20, transcendentals=4096),
    )(colour, own, opposite, left, right)


def half(matrix, colour):
    return lax.dynamic_slice_in_dim(matrix, colour * 512, 512, axis=1)


def body(passages, norm_gain, w_key, w_value, queries, lengths, passage_question):
    cat = lambda parts: jnp.concatenate(parts, axis=0)
    enc, x, core = lax.axis_index("enc"), lax.axis_index("dec"), lax.axis_index("mdl")
    y, z = enc // NZ, enc % NZ
    colour = x % 2
    pass_local, slot_count, width = passages.shape
    token_count = pass_local * slot_count

    mine = jnp.concatenate([half(w_key, colour), half(w_value, colour)], axis=1)
    theirs = jnp.concatenate([half(w_key, 1 - colour), half(w_value, 1 - colour)], axis=1)
    ring = [mine, shift_x(theirs, -1), shift_x(mine, 2), shift_x(theirs, 1)]
    rows = lax.dynamic_slice_in_dim(cat(ring + ring[:3]), (NX - x) % NX * 32, 128, axis=0)

    order = jnp.stack([(y + dy) % NY * NZ + (z + dz) % NZ for dy in DY for dz in DZ]).astype(jnp.int32)
    own = normalise(order, passages.reshape(token_count, width), norm_gain.reshape(1, width))
    outgoing = lax.dynamic_slice_in_dim(own, core * TILE, TILE, axis=0)
    rows, outgoing = lax.optimization_barrier((rows, outgoing))
    near = split_x(outgoing)

    value_rows, key_rows = rows[:, 512:], rows[:, :512]
    v0 = cat([value_rows, shift_y(value_rows, 1), shift_y(value_rows, -1), shift_y(value_rows, 2)])
    vr1, vl1 = shift_z(v0, 1), shift_z(v0, -1)
    kr1, kl1 = shift_z(key_rows, 1), shift_z(key_rows, -1)
    kr2, kl2 = shift_z(kr1, 1), shift_z(kl1, -1)
    kr3, kl3 = shift_z(kr2, 1), shift_z(kl2, -1)
    kr4, kl4 = shift_z(kr3[:64], 1), shift_z(kl3[64:], -1)
    k0 = cat([key_rows, kr1, kr2, kr3, kl1, kl2, kl3, kr4, kl4])
    vr2, vl2 = shift_z(vr1, 1), shift_z(vl1, -1)
    ky1, ky3 = shift_y(k0, 1), shift_y(k0, -1)
    vr3, vl3 = shift_z(vr2, 1), shift_z(vl2, -1)
    vr4, vl4 = shift_z(vr3[:256], 1), shift_z(vl3[256:], -1)
    ky2a, ky2b = shift_y(ky1[:512], 1), shift_y(ky3[512:], -1)

    near_late, _ = lax.optimization_barrier((near, kr4))
    far = other_core(near_late)

    facts = jnp.concatenate([lengths, passage_question - enc * 2]).reshape(1, 6)
    facts, _ = lax.optimization_barrier((facts, kr1))
    low, high = shift_x(facts, 1)[0], shift_x(facts, -1)[0]
    facts = facts[0]

    def units(facts, chosen):
        live = jnp.stack([facts[p] - at for p, at in chosen])
        return live, jnp.stack([facts[3 + p] for p, _ in chosen])

    every = [(p, at) for p in range(3) for at in (0, 128)]
    own_live, own_owner = units(facts, every)
    low_live, low_owner = units(low, every[:3])
    high_live, high_owner = units(high, every[3:])
    flip = lambda a, b: jnp.where(core == 0, jnp.concatenate([a, b]), jnp.concatenate([b, a]))
    live = jnp.concatenate([own_live, flip(low_live, high_live)]).astype(jnp.int32)
    owner = jnp.concatenate([own_owner, flip(low_owner, high_owner)]).astype(jnp.int32)

    rows_q = half(queries.reshape(128, -1), colour).reshape(2, 64, 2, 4, HD)
    turned = jnp.transpose(rows_q, (0, 2, 3, 4, 1))
    eye = jnp.eye(4, dtype=jnp.bool_)[None, None, :, None, :, None]
    blocks = jnp.where(eye, turned[:, :, :, :, None, :], jnp.zeros((), jnp.bfloat16))
    blocks = blocks.reshape(4, 256, 256)

    key_acc, value_acc, rest = project(
        own, near_late, far, (k0, ky1, ky3), (v0, vr1, vr2, vr3, vl1, vl2, vl3)
    )
    part = attend(owner, live, key_acc, value_acc, rest, (ky2a, ky2b), (vr4, vl4), blocks)
    result = combine(
        colour.reshape(1).astype(jnp.int32),
        part,
        shift_x(part, 2),
        shift_x(part, 1),
        shift_x(part, -1),
    )
    return result.reshape(2, 64, 1024)


def solution(mesh):
    return jax.shard_map(
        body,
        mesh=mesh,
        in_specs=(
            P(("enc", "dec"), None, None),
            P(),
            P(("enc", "dec"), "mdl"),
            P(("enc", "dec"), "mdl"),
            P("enc", None, "mdl"),
            P(("enc", "dec")),
            P(("enc", "dec")),
        ),
        out_specs=P("enc", None, "mdl"),
        check_vma=False,
    )
```

time: 335 us -> 204 us (0.61)
  the two profiles are of different devices: /device:TPU:1 before, /device:TPU:6 now
where the time goes in v1:
time: 204 us; the launch traced here: 203 us
  starting transfers between devices  54.9 us (27%)
  waiting for transfers between devices  52.2 us (26%)
  local copies, waits for them, and re-layouts  47.6 us (23%)
  Pallas kernels  40.9 us (20%)
  between operations  4.01 us (2%)
  other arithmetic  2.87 us (1%)
    ppermute x16, waiting for transfers between devices, shift_z(): return lax.ppermute(value, 'enc', pairs)  35.6 us
    ppermute x16, starting transfers between devices, shift_z(): return lax.ppermute(value, 'enc', pairs)  26.9 us
    pallas_call x1, Pallas kernels, project(): pl.pallas_call(project_kernel, out_shape=(jax.ShapeDtypeStruct((rows, col...  19 us
    unnamed x49, local copies, waits for them, and re-layouts  14.2 us
    ppermute x7, starting transfers between devices, shift_y(): return lax.ppermute(value, 'enc', pairs)  13.9 us
    ppermute x8, starting transfers between devices, shift_x(): return lax.ppermute(value, 'dec', [(x, (x + step) % NX) for x in range(NX)])  12.1 us
    pallas_call x1, Pallas kernels, attend(): pl.pallas_call(attend_kernel, out_shape=jax.ShapeDtypeStruct((8, 80, 128)...  10.9 us
    pallas_call x1, Pallas kernels, normalise(): pl.pallas_call(norm_kernel, out_shape=jax.ShapeDtypeStruct((rows, width),...  8.89 us
  transfers between devices with their start and end apart: 33, of which 14 were waited for; matrix products, arithmetic and copies ran while one was open for 21% of the time, Pallas kernels for 14%

profile of v1, /device:TPU:6, one launch (start us, length us, event | category | flops | bytes accessed | tf_op | source)
XLA Modules:
  0.0 202.5 jit_solution(13654328514773826725)
XLA Ops:
  2.3 2.4 %collective-permute-start.2 = (bf16[32,1024]{1,0:T(8,128)(2,1)}, bf16[32,1024]{1,0:T(8,128)(2,1)}, u32[]{:S(2)}, u32[]{:S(2)}) collective-permute-start(bf16[32,1024]{1,0:T(8,128)(2,1)} %pad_maximum_fusion.1), channel_id=1, source_target_pairs={{0,2},{2,4},{4,6},{6,0},{1,3},{3,5},{5,7},{7,1},{8,10},{10,12},{12... | collective-permute-start | bytes 196616 | tf_op jit(solution)/shard_map/ppermute | solution.py:31
  5.8 1.3 reshape.73.gain_ref
  7.9 8.9 %shard_map.73.own_ref = bf16[768,4096]{1,0:T(8,128)(2,1)} custom-call(s32[32]{0:T(128)} %stack.153.order_ref, bf16[768,4096]{1,0:T(8,128)(2,1)} %bitcast.59, bf16[1,4096]{1,0:T(2,128)(2,1)} %reshape.73.gain_ref), custom_call_target="tpu_custom_call" | custom-call | flops 18874368 | bytes 12582912 | tf_op jit(solution)/shard_map/pallas_call | solution.py:58
  16.7 2.1 %constant_dynamic-slice_fusion.1 = bf16[384,4096]{1,0:T(8,128)(2,1)S(1)} fusion(bf16[768,4096]{1,0:T(8,128)(2,1)} %shard_map.73.own_ref, s32[]{:T(128)S(6)} %select_n.222), kind=kLoop, calls=%fused_computation.22 | loop fusion | bytes 6291460 | tf_op jit(solution)/shard_map/dynamic_slice | solution.py:293
  19.5 1.5 constant_dynamic-update-slice_fusion.4
  21.0 1.5 constant_dynamic-update-slice_fusion.3
  23.7 1.5 constant_dynamic-update-slice_fusion
  26.2 1.9 collective-permute-start.6
  28.8 1.9 collective-permute-start.3
  30.7 6.9 %collective-permute-done.3 = bf16[128,512]{1,0:T(8,128)(2,1)S(1)} collective-permute-done((bf16[128,512]{1,0:T(8,128)(2,1)S(1)}, bf16[128,512]{1,0:T(8,128)(2,1)S(1)}, u32[]{:S(2)}, u32[]{:S(2)}) %collective-permute-start.3) | collective-permute-done | bytes 131104 | tf_op jit(solution)/shard_map/ppermute | solution.py:22
  37.6 6.9 %collective-permute-done.7 = bf16[128,512]{1,0:T(8,128)(2,1)S(1)} collective-permute-done((bf16[128,512]{1,0:T(8,128)(2,1)S(1)}, bf16[128,512]{1,0:T(8,128)(2,1)S(1)}, u32[]{:S(2)}, u32[]{:S(2)}) %collective-permute-start.7) | collective-permute-done | bytes 131104 | tf_op jit(solution)/shard_map/ppermute | solution.py:22
  44.4 6.5 %collective-permute-done.8 = bf16[128,512]{1,0:T(8,128)(2,1)S(1)} collective-permute-done((bf16[128,512]{1,0:T(8,128)(2,1)S(1)}, bf16[128,512]{1,0:T(8,128)(2,1)S(1)}, u32[]{:S(2)}, u32[]{:S(2)}) %collective-permute-start.8) | collective-permute-done | bytes 131104 | tf_op jit(solution)/shard_map/ppermute | solution.py:22
  51.1 5.5 %collective-permute-done.9 = bf16[64,512]{1,0:T(8,128)(2,1)S(1)} collective-permute-done((bf16[64,512]{1,0:T(8,128)(2,1)S(1)}, bf16[64,512]{1,0:T(8,128)(2,1)S(1)}, u32[]{:S(2)}, u32[]{:S(2)}) %collective-permute-start.9) | collective-permute-done | bytes 65568 | tf_op jit(solution)/shard_map/ppermute | solution.py:22
  56.5 7.1 %collective-permute-done.6.near_ref = bf16[384,4096]{1,0:T(8,128)(2,1)} collective-permute-done((bf16[384,4096]{1,0:T(8,128)(2,1)S(1)}, bf16[384,4096]{1,0:T(8,128)(2,1)}, u32[]{:S(2)}, u32[]{:S(2)}) %collective-permute-start.6) | collective-permute-done | bytes 3145760 | tf_op jit(solution)/shard_map/ppermute | solution.py:38
  63.7 5.7 %collective-permute-start.11 = (bf16[128,512]{1,0:T(8,128)(2,1)}, bf16[128,512]{1,0:T(8,128)(2,1)S(1)}, u32[]{:S(2)}, u32[]{:S(2)}) collective-permute-start(bf16[128,512]{1,0:T(8,128)(2,1)} %copy-done.6), channel_id=1, source_target_pairs={{0,56},{8,0},{16,8},{24,16},{32,24},{40,32},{48,40},{56,48},{64,12... | collective-permute-start | bytes 393224 | tf_op jit(solution)/shard_map/ppermute | solution.py:22
  69.4 3.2 %collective-permute-start.19 = (bf16[128,512]{1,0:T(8,128)(2,1)S(1)}, bf16[128,512]{1,0:T(8,128)(2,1)S(1)}, u32[]{:S(2)}, u32[]{:S(2)}) collective-permute-start(bf16[128,512]{1,0:T(8,128)(2,1)S(1)} %get-tuple-element.19), channel_id=1, source_target_pairs={{0,128},{8,136},{16,144},{24,152},{32,160},{40,168},{48,176},{56,1... | collective-permute-start | bytes 393224 | tf_op jit(solution)/shard_map/ppermute | solution.py:27
  74.7 2.0 collective-permute-start.12
  77.1 2.5 %collective-permute-done.18 = bf16[128,512]{1,0:T(8,128)(2,1)S(1)} collective-permute-done((bf16[128,512]{1,0:T(8,128)(2,1)S(1)}, bf16[128,512]{1,0:T(8,128)(2,1)S(1)}, u32[]{:S(2)}, u32[]{:S(2)}) %collective-permute-start.18) | collective-permute-done | bytes 131104 | tf_op jit(solution)/shard_map/ppermute | solution.py:27
  80.2 3.2 %collective-permute-start.23 = (bf16[512,512]{1,0:T(8,128)(2,1)S(1)}, bf16[512,512]{1,0:T(8,128)(2,1)}, u32[]{:S(2)}, u32[]{:S(2)}) collective-permute-start(bf16[512,512]{1,0:T(8,128)(2,1)S(1)} %pad_maximum_fusion.refs_3_), channel_id=1, source_target_pairs={{0,56},{8,0},{16,8},{24,16},{32,24},{40,32},{48,40},{56,48},{64,12... | collective-permute-start | bytes 1572872 | tf_op jit(solution)/shard_map/ppermute | solution.py:22
  83.5 3.3 %collective-permute-start.4 = (s32[1,6]{1,0:T(1,128)S(1)}, s32[1,6]{1,0:T(1,128)S(1)}, u32[]{:S(2)}, u32[]{:S(2)}) collective-permute-start(s32[1,6]{1,0:T(1,128)S(1)} %add_bitcast_fusion), channel_id=1, source_target_pairs={{0,2},{2,4},{4,6},{6,0},{1,3},{3,5},{5,7},{7,1},{8,10},{10,12},{12... | collective-permute-start | bytes 80 | tf_op jit(solution)/shard_map/ppermute | solution.py:31
  86.8 1.6 constant_dynamic-update-slice_fusion.14
  88.4 1.6 constant_dynamic-update-slice_fusion.13
  89.9 6.5 %collective-permute-done.13 = bf16[128,512]{1,0:T(8,128)(2,1)S(1)} collective-permute-done((bf16[128,512]{1,0:T(8,128)(2,1)S(1)}, bf16[128,512]{1,0:T(8,128)(2,1)S(1)}, u32[]{:S(2)}, u32[]{:S(2)}) %collective-permute-start.13) | collective-permute-done | bytes 131104 | tf_op jit(solution)/shard_map/ppermute | solution.py:22
  96.4 3.7 %collective-permute-start.14 = (bf16[64,512]{1,0:T(8,128)(2,1)S(1)}, bf16[64,512]{1,0:T(8,128)(2,1)S(1)}, u32[]{:S(2)}, u32[]{:S(2)}) collective-permute-start(bf16[64,512]{1,0:T(8,128)(2,1)S(1)} %slice.152), channel_id=1, source_target_pairs={{0,56},{8,0},{16,8},{24,16},{32,24},{40,32},{48,40},{56,48},{64,12... | collective-permute-start | bytes 196616 | tf_op jit(solution)/shard_map/ppermute | solution.py:22
  100.1 1.6 constant_dynamic-update-slice_fusion.12
  103.7 1.5 constant_dynamic-update-slice_fusion.8
  105.1 1.3 collective-permute-start.5
  107.0 1.9 collective-permute-start.15
  110.0 3.4 %collective-permute-start.16 = (bf16[1024,512]{1,0:T(8,128)(2,1)}, bf16[1024,512]{1,0:T(8,128)(2,1)}, u32[]{:S(2)}, u32[]{:S(2)}) collective-permute-start(bf16[1024,512]{1,0:T(8,128)(2,1)} %constant_dynamic-update-slice_fusion.7.refs_0_), channel_id=1, source_target_pairs={{0,192},{8,200},{16,208},{24,216},{32,224},{40,232},{48,240},{56,2... | collective-permute-start | bytes 3145736 | tf_op jit(solution)/shard_map/ppermute | solution.py:27
  113.4 3.2 %collective-permute-start.24 = (bf16[512,512]{1,0:T(8,128)(2,1)}, bf16[512,512]{1,0:T(8,128)(2,1)}, u32[]{:S(2)}, u32[]{:S(2)}) collective-permute-start(bf16[512,512]{1,0:T(8,128)(2,1)} %collective-permute-done.23.refs_7_), channel_id=1, source_target_pairs={{0,56},{8,0},{16,8},{24,16},{32,24},{40,32},{48,40},{56,48},{64,12... | collective-permute-start | bytes 1572872 | tf_op jit(solution)/shard_map/ppermute | solution.py:22
  122.5 3.4 %collective-permute-done.21.refs_5_ = bf16[512,512]{1,0:T(8,128)(2,1)} collective-permute-done((bf16[512,512]{1,0:T(8,128)(2,1)S(1)}, bf16[512,512]{1,0:T(8,128)(2,1)}, u32[]{:S(2)}, u32[]{:S(2)}) %collective-permute-start.21) | collective-permute-done | bytes 524320 | tf_op jit(solution)/shard_map/ppermute | solution.py:22
  125.9 3.2 %collective-permute-start.25 = (bf16[512,512]{1,0:T(8,128)(2,1)}, bf16[512,512]{1,0:T(8,128)(2,1)S(1)}, u32[]{:S(2)}, u32[]{:S(2)}) collective-permute-start(bf16[512,512]{1,0:T(8,128)(2,1)} %collective-permute-done.24.refs_8_), channel_id=1, source_target_pairs={{0,56},{8,0},{16,8},{24,16},{32,24},{40,32},{48,40},{56,48},{64,12... | collective-permute-start | bytes 1572872 | tf_op jit(solution)/shard_map/ppermute | solution.py:22
  129.8 4.0 %concatenate.44 = s32[6]{0:T(128)S(1)} concatenate(s32[1]{0:T(128)} %bitcast.38, s32[1]{0:T(128)} %bitcast.38, s32[1]{0:T(128)} %bitcast.39, s32[1]{0:T(128)} %bitcast.40, s32[1]{0:T(128)} %bitcast.41, s32[1]{0:T(128)} %bitcast.41), dimensions={0} | concatenate | bytes 48 | tf_op jit(solution)/shard_map/concatenate | solution.py:327
  133.8 4.0 %concatenate.45 = s32[6]{0:T(128)S(1)} concatenate(s32[1]{0:T(128)} %bitcast.40, s32[1]{0:T(128)} %bitcast.41, s32[1]{0:T(128)} %bitcast.41, s32[1]{0:T(128)} %bitcast.38, s32[1]{0:T(128)} %bitcast.38, s32[1]{0:T(128)} %bitcast.39), dimensions={0} | concatenate | bytes 48 | tf_op jit(solution)/shard_map/concatenate | solution.py:327
  139.6 1.8 concatenate.47
  141.4 1.8 concatenate.48
  143.3 4.4 %concatenate.46.owner_ref = s32[12]{0:T(128)} concatenate(s32[1]{0:T(128)} %bitcast.35, s32[1]{0:T(128)} %bitcast.35, s32[1]{0:T(128)} %bitcast.36, s32[1]{0:T(128)} %bitcast.36, s32[1]{0:T(128)} %bitcast.37, s32[1]{0:T(128)} %bitcast.37, s32[6]{0:T(128)S(1)} %broadcast_select_fusion.2), dimensions={0} | concatenate | bytes 96 | tf_op jit(solution)/shard_map/concatenate | solution.py:329
  147.7 2.5 %concatenate.49.live_ref = s32[12]{0:T(128)} concatenate(s32[1]{0:T(128)} %bitcast.42, s32[1]{0:T(128)} %bitcast.43, s32[1]{0:T(128)} %bitcast.44, s32[1]{0:T(128)} %bitcast.45, s32[1]{0:T(128)} %bitcast.46, s32[1]{0:T(128)} %bitcast.47, s32[6]{0:T(128)S(1)} %broadcast_select_fusion.1), dimensions={0} | concatenate | bytes 96 | tf_op jit(solution)/shard_map/concatenate | solution.py:328
  151.4 1.1 slice.154
  152.5 3.3 %collective-permute-start.27 = (bf16[512,512]{1,0:T(8,128)(2,1)S(1)}, bf16[512,512]{1,0:T(8,128)(2,1)S(1)}, u32[]{:S(2)}, u32[]{:S(2)}) collective-permute-start(bf16[512,512]{1,0:T(8,128)(2,1)S(1)} %slice.154), channel_id=1, source_target_pairs={{0,192},{8,200},{16,208},{24,216},{32,224},{40,232},{48,240},{56,2... | collective-permute-start | bytes 1572872 | tf_op jit(solution)/shard_map/ppermute | solution.py:27
  156.1 3.3 %collective-permute-start.29 = (bf16[256,512]{1,0:T(8,128)(2,1)S(1)}, bf16[256,512]{1,0:T(8,128)(2,1)S(1)}, u32[]{:S(2)}, u32[]{:S(2)}) collective-permute-start(bf16[256,512]{1,0:T(8,128)(2,1)S(1)} %slice.156), channel_id=1, source_target_pairs={{0,56},{8,0},{16,8},{24,16},{32,24},{40,32},{48,40},{56,48},{64,12... | collective-permute-start | bytes 786440 | tf_op jit(solution)/shard_map/ppermute | solution.py:22
  159.4 19.0 %shard_map.74 = (f32[1536,512]{1,0:T(8,128)}, f32[1536,512]{1,0:T(8,128)}, bf16[1536,1536]{1,0:T(8,128)(2,1)}) custom-call(bf16[768,4096]{1,0:T(8,128)(2,1)} %shard_map.73.own_ref, bf16[384,4096]{1,0:T(8,128)(2,1)} %collective-permute-done.6.near_ref, bf16[384,4096]{1,0:T(8,128)(2,1)} %collective-permute-done.10.far_ref, ...), custom_call_target="tpu_custom_call" | custom-call | flops 10468982784 | bytes 25690112 | tf_op jit(solution)/shard_map/pallas_call | solution.py:116
  179.6 10.9 %shard_map.75.own = bf16[8,80,128]{2,1,0:T(8,128)(2,1)} custom-call(s32[12]{0:T(128)} %concatenate.46.owner_ref, s32[12]{0:T(128)} %concatenate.49.live_ref, f32[1536,512]{1,0:T(8,128)} %get-tuple-element.16.key_acc, f32[1536,512]{1,0:T(8,128)} %get-tuple-element.17.value_acc, bf16[1536,1536]{1,0:T(8,128)(2,1)} %get-tuple-element.18.rest_ref, ...), custom_call_target="tpu_custom_call" | custom-call | flops 4026531840 | bytes 12582912 | tf_op jit(solution)/shard_map/pallas_call | solution.py:213
  190.5 1.8 collective-permute-start.30
  193.0 1.3 collective-permute-start.32
  194.3 3.2 %collective-permute-done.30.opposite = bf16[8,80,128]{2,1,0:T(8,128)(2,1)S(1)} collective-permute-done((bf16[8,80,128]{2,1,0:T(8,128)(2,1)}, bf16[8,80,128]{2,1,0:T(8,128)(2,1)S(1)}, u32[]{:S(2)}, u32[]{:S(2)}) %collective-permute-start.30) | collective-permute-done | bytes 163872 | tf_op jit(solution)/shard_map/ppermute | solution.py:31
  198.4 1.3 collective-permute-done.32.right
  200.4 2.1 %shard_map.76 = bf16[128,1024]{1,0:T(8,128)(2,1)} custom-call(s32[1]{0:T(128)} %bitcast.colour_ref, bf16[8,80,128]{2,1,0:T(8,128)(2,1)} %shard_map.75.own, bf16[8,80,128]{2,1,0:T(8,128)(2,1)} %copy-done.3, bf16[8,80,128]{2,1,0:T(8,128)(2,1)} %copy-done.4, bf16[8,80,128]{2,1,0:T(8,128)(2,1)} %copy-done.5), custom_call_target="tpu_custom_call" | custom-call | flops 1048576 | bytes 1048576 | tf_op jit(solution)/shard_map/pallas_call | solution.py:263
  (111 shorter events, 24.2 us)
Async XLA Ops:
  0.0 74.7 %copy-start = (bf16[2,64,1024]{2,1,0:T(8,128)(2,1)S(1)}, bf16[2,64,1024]{2,1,0:T(8,128)(2,1)}, u32[]{:S(2)}) copy-start(bf16[2,64,1024]{2,1,0:T(8,128)(2,1)} %param.11) | copy-start | bytes 786436
  1.5 17.4 %collective-permute-start = (bf16[32,1024]{1,0:T(8,128)(2,1)}, bf16[32,1024]{1,0:T(8,128)(2,1)S(1)}, u32[]{:S(2)}, u32[]{:S(2)}) collective-permute-start(bf16[32,1024]{1,0:T(8,128)(2,1)} %pad_maximum_fusion.1), channel_id=1, source_target_pairs={{0,6},{2,0},{4,2},{6,4},{1,7},{3,1},{5,3},{7,5},{8,14},{10,8},{12,... | collective-permute-start | bytes 196616 | tf_op jit(solution)/shard_map/ppermute | solution.py:31
  2.3 18.7 %collective-permute-start.2 = (bf16[32,1024]{1,0:T(8,128)(2,1)}, bf16[32,1024]{1,0:T(8,128)(2,1)}, u32[]{:S(2)}, u32[]{:S(2)}) collective-permute-start(bf16[32,1024]{1,0:T(8,128)(2,1)} %pad_maximum_fusion.1), channel_id=1, source_target_pairs={{0,2},{2,4},{4,6},{6,0},{1,3},{3,5},{5,7},{7,1},{8,10},{10,12},{12... | collective-permute-start | bytes 196616 | tf_op jit(solution)/shard_map/ppermute | solution.py:31
  5.4 14.1 %collective-permute-start.1 = (bf16[32,1024]{1,0:T(8,128)(2,1)}, bf16[32,1024]{1,0:T(8,128)(2,1)}, u32[]{:S(2)}, u32[]{:S(2)}) collective-permute-start(bf16[32,1024]{1,0:T(8,128)(2,1)} %get-tuple-element.22), channel_id=1, source_target_pairs={{0,4},{2,6},{4,0},{6,2},{1,5},{3,7},{5,1},{7,3},{8,12},{10,14},{12... | collective-permute-start | bytes 196616 | tf_op jit(solution)/shard_map/ppermute | solution.py:31
  16.7 52.7 %copy-start.17 = (s32[3]{0:T(128)S(1)}, s32[3]{0:T(128)}, u32[]{:S(2)}) copy-start(s32[3]{0:T(128)} %param.13) | copy-start | bytes 40
  16.7 60.0 %copy-start.18 = (s32[3]{0:T(128)S(1)}, s32[3]{0:T(128)}, u32[]{:S(2)}) copy-start(s32[3]{0:T(128)} %param.12) | copy-start | bytes 40
  26.2 37.5 %collective-permute-start.6 = (bf16[384,4096]{1,0:T(8,128)(2,1)S(1)}, bf16[384,4096]{1,0:T(8,128)(2,1)}, u32[]{:S(2)}, u32[]{:S(2)}) collective-permute-start(bf16[384,4096]{1,0:T(8,128)(2,1)S(1)} %constant_dynamic-slice_fusion.1), channel_id=1, source_target_pairs={{0,2},{1,7},{2,4},{3,1},{4,6},{5,3},{6,0},{7,5},{8,10},{9,15},{10,... | collective-permute-start | bytes 9437192 | tf_op jit(solution)/shard_map/ppermute | solution.py:38
  28.8 34.9 %copy-start.6 = (bf16[128,512]{1,0:T(8,128)(2,1)}, bf16[128,512]{1,0:T(8,128)(2,1)S(1)}, u32[]{:S(2)}) copy-start(bf16[128,512]{1,0:T(8,128)(2,1)S(1)} %get-tuple-element.21) | copy-start | bytes 393220
  28.8 8.8 %collective-permute-start.3 = (bf16[128,512]{1,0:T(8,128)(2,1)S(1)}, bf16[128,512]{1,0:T(8,128)(2,1)S(1)}, u32[]{:S(2)}, u32[]{:S(2)}) collective-permute-start(bf16[128,512]{1,0:T(8,128)(2,1)S(1)} %get-tuple-element.21), channel_id=1, source_target_pairs={{0,8},{8,16},{16,24},{24,32},{32,40},{40,48},{48,56},{56,0},{64,72... | collective-permute-start | bytes 393224 | tf_op jit(solution)/shard_map/ppermute | solution.py:22
  37.6 6.9 %copy-start.9 = (bf16[128,512]{1,0:T(8,128)(2,1)}, bf16[128,512]{1,0:T(8,128)(2,1)S(1)}, u32[]{:S(2)}) copy-start(bf16[128,512]{1,0:T(8,128)(2,1)S(1)} %collective-permute-done.3) | copy-start | bytes 393220
  37.6 6.9 %collective-permute-start.7 = (bf16[128,512]{1,0:T(8,128)(2,1)S(1)}, bf16[128,512]{1,0:T(8,128)(2,1)S(1)}, u32[]{:S(2)}, u32[]{:S(2)}) collective-permute-start(bf16[128,512]{1,0:T(8,128)(2,1)S(1)} %collective-permute-done.3), channel_id=1, source_target_pairs={{0,8},{8,16},{16,24},{24,32},{32,40},{40,48},{48,56},{56,0},{64,72... | collective-permute-start | bytes 393224 | tf_op jit(solution)/shard_map/ppermute | solution.py:22
  44.4 19.2 %copy-start.10 = (bf16[128,512]{1,0:T(8,128)(2,1)}, bf16[128,512]{1,0:T(8,128)(2,1)S(1)}, u32[]{:S(2)}) copy-start(bf16[128,512]{1,0:T(8,128)(2,1)S(1)} %collective-permute-done.7) | copy-start | bytes 393220
  44.4 6.5 %collective-permute-start.8 = (bf16[128,512]{1,0:T(8,128)(2,1)S(1)}, bf16[128,512]{1,0:T(8,128)(2,1)S(1)}, u32[]{:S(2)}, u32[]{:S(2)}) collective-permute-start(bf16[128,512]{1,0:T(8,128)(2,1)S(1)} %collective-permute-done.7), channel_id=1, source_target_pairs={{0,8},{8,16},{16,24},{24,32},{32,40},{40,48},{48,56},{56,0},{64,72... | collective-permute-start | bytes 393224 | tf_op jit(solution)/shard_map/ppermute | solution.py:22
  51.0 12.6 %copy-start.2 = (bf16[128,512]{1,0:T(8,128)(2,1)}, bf16[128,512]{1,0:T(8,128)(2,1)S(1)}, u32[]{:S(2)}) copy-start(bf16[128,512]{1,0:T(8,128)(2,1)S(1)} %collective-permute-done.8) | copy-start | bytes 393220
  51.0 5.6 %collective-permute-start.9 = (bf16[64,512]{1,0:T(8,128)(2,1)S(1)}, bf16[64,512]{1,0:T(8,128)(2,1)S(1)}, u32[]{:S(2)}, u32[]{:S(2)}) collective-permute-start(bf16[64,512]{1,0:T(8,128)(2,1)S(1)} %slice.151), channel_id=1, source_target_pairs={{0,8},{8,16},{16,24},{24,32},{32,40},{40,48},{48,56},{56,0},{64,72... | collective-permute-start | bytes 196616 | tf_op jit(solution)/shard_map/ppermute | solution.py:22
  56.5 7.1 %copy-start.11 = (bf16[64,512]{1,0:T(8,128)(2,1)}, bf16[64,512]{1,0:T(8,128)(2,1)S(1)}, u32[]{:S(2)}) copy-start(bf16[64,512]{1,0:T(8,128)(2,1)S(1)} %collective-permute-done.9) | copy-start | bytes 196612
  63.6 95.8 %collective-permute-start.10 = (bf16[384,4096]{1,0:T(8,128)(2,1)}, bf16[384,4096]{1,0:T(8,128)(2,1)}, u32[]{:S(2)}, u32[]{:S(2)}) collective-permute-start(bf16[384,4096]{1,0:T(8,128)(2,1)} %collective-permute-done.6.near_ref), channel_id=1, source_target_pairs={{0,1},{1,0},{2,3},{3,2},{4,5},{5,4},{6,7},{7,6},{8,9},{9,8},{10,11... | collective-permute-start | bytes 9437192 | tf_op jit(solution)/shard_map/ppermute | solution.py:42
  63.7 10.9 %collective-permute-start.11 = (bf16[128,512]{1,0:T(8,128)(2,1)}, bf16[128,512]{1,0:T(8,128)(2,1)S(1)}, u32[]{:S(2)}, u32[]{:S(2)}) collective-permute-start(bf16[128,512]{1,0:T(8,128)(2,1)} %copy-done.6), channel_id=1, source_target_pairs={{0,56},{8,0},{16,8},{24,16},{32,24},{40,32},{48,40},{56,48},{64,12... | collective-permute-start | bytes 393224 | tf_op jit(solution)/shard_map/ppermute | solution.py:22
  69.4 7.7 %collective-permute-start.19 = (bf16[128,512]{1,0:T(8,128)(2,1)S(1)}, bf16[128,512]{1,0:T(8,128)(2,1)S(1)}, u32[]{:S(2)}, u32[]{:S(2)}) collective-permute-start(bf16[128,512]{1,0:T(8,128)(2,1)S(1)} %get-tuple-element.19), channel_id=1, source_target_pairs={{0,128},{8,136},{16,144},{24,152},{32,160},{40,168},{48,176},{56,1... | collective-permute-start | bytes 393224 | tf_op jit(solution)/shard_map/ppermute | solution.py:27
  72.6 7.0 %collective-permute-start.18 = (bf16[128,512]{1,0:T(8,128)(2,1)S(1)}, bf16[128,512]{1,0:T(8,128)(2,1)S(1)}, u32[]{:S(2)}, u32[]{:S(2)}) collective-permute-start(bf16[128,512]{1,0:T(8,128)(2,1)S(1)} %get-tuple-element.19), channel_id=1, source_target_pairs={{0,192},{8,200},{16,208},{24,216},{32,224},{40,232},{48,240},{56,2... | collective-permute-start | bytes 393224 | tf_op jit(solution)/shard_map/ppermute | solution.py:27
  73.7 6.2 %collective-permute-start.17 = (bf16[128,512]{1,0:T(8,128)(2,1)S(1)}, bf16[128,512]{1,0:T(8,128)(2,1)S(1)}, u32[]{:S(2)}, u32[]{:S(2)}) collective-permute-start(bf16[128,512]{1,0:T(8,128)(2,1)S(1)} %get-tuple-element.19), channel_id=1, source_target_pairs={{0,64},{8,72},{16,80},{24,88},{32,96},{40,104},{48,112},{56,120},{... | collective-permute-start | bytes 393224 | tf_op jit(solution)/shard_map/ppermute | solution.py:27
  74.7 12.1 %collective-permute-start.12 = (bf16[128,512]{1,0:T(8,128)(2,1)S(1)}, bf16[128,512]{1,0:T(8,128)(2,1)S(1)}, u32[]{:S(2)}, u32[]{:S(2)}) collective-permute-start(bf16[128,512]{1,0:T(8,128)(2,1)S(1)} %collective-permute-done.11), channel_id=1, source_target_pairs={{0,56},{8,0},{16,8},{24,16},{32,24},{40,32},{48,40},{56,48},{64,12... | collective-permute-start | bytes 393224 | tf_op jit(solution)/shard_map/ppermute | solution.py:22
  80.0 39.4 %copy-start.1 = (bf16[512,512]{1,0:T(8,128)(2,1)}, bf16[512,512]{1,0:T(8,128)(2,1)S(1)}, u32[]{:S(2)}) copy-start(bf16[512,512]{1,0:T(8,128)(2,1)S(1)} %pad_maximum_fusion.refs_3_) | copy-start | bytes 1572868
  80.0 33.4 %collective-permute-start.20 = (bf16[512,512]{1,0:T(8,128)(2,1)S(1)}, bf16[512,512]{1,0:T(8,128)(2,1)S(1)}, u32[]{:S(2)}, u32[]{:S(2)}) collective-permute-start(bf16[512,512]{1,0:T(8,128)(2,1)S(1)} %pad_maximum_fusion.refs_3_), channel_id=1, source_target_pairs={{0,8},{8,16},{16,24},{24,32},{32,40},{40,48},{48,56},{56,0},{64,72... | collective-permute-start | bytes 1572872 | tf_op jit(solution)/shard_map/ppermute | solution.py:22
  80.2 33.1 %collective-permute-start.23 = (bf16[512,512]{1,0:T(8,128)(2,1)S(1)}, bf16[512,512]{1,0:T(8,128)(2,1)}, u32[]{:S(2)}, u32[]{:S(2)}) collective-permute-start(bf16[512,512]{1,0:T(8,128)(2,1)S(1)} %pad_maximum_fusion.refs_3_), channel_id=1, source_target_pairs={{0,56},{8,0},{16,8},{24,16},{32,24},{40,32},{48,40},{56,48},{64,12... | collective-permute-start | bytes 1572872 | tf_op jit(solution)/shard_map/ppermute | solution.py:22
  83.5 23.6 %collective-permute-start.4 = (s32[1,6]{1,0:T(1,128)S(1)}, s32[1,6]{1,0:T(1,128)S(1)}, u32[]{:S(2)}, u32[]{:S(2)}) collective-permute-start(s32[1,6]{1,0:T(1,128)S(1)} %add_bitcast_fusion), channel_id=1, source_target_pairs={{0,2},{2,4},{4,6},{6,0},{1,3},{3,5},{5,7},{7,1},{8,10},{10,12},{12... | collective-permute-start | bytes 80 | tf_op jit(solution)/shard_map/ppermute | solution.py:31
  86.8 9.6 %collective-permute-start.13 = (bf16[128,512]{1,0:T(8,128)(2,1)S(1)}, bf16[128,512]{1,0:T(8,128)(2,1)S(1)}, u32[]{:S(2)}, u32[]{:S(2)}) collective-permute-start(bf16[128,512]{1,0:T(8,128)(2,1)S(1)} %collective-permute-done.12), channel_id=1, source_target_pairs={{0,56},{8,0},{16,8},{24,16},{32,24},{40,32},{48,40},{56,48},{64,12... | collective-permute-start | bytes 393224 | tf_op jit(solution)/shard_map/ppermute | solution.py:22
  96.4 8.7 %collective-permute-start.14 = (bf16[64,512]{1,0:T(8,128)(2,1)S(1)}, bf16[64,512]{1,0:T(8,128)(2,1)S(1)}, u32[]{:S(2)}, u32[]{:S(2)}) collective-permute-start(bf16[64,512]{1,0:T(8,128)(2,1)S(1)} %slice.152), channel_id=1, source_target_pairs={{0,56},{8,0},{16,8},{24,16},{32,24},{40,32},{48,40},{56,48},{64,12... | collective-permute-start | bytes 196616 | tf_op jit(solution)/shard_map/ppermute | solution.py:22
  105.1 4.8 %collective-permute-start.5 = (s32[1,6]{1,0:T(1,128)S(1)}, s32[1,6]{1,0:T(1,128)S(1)}, u32[]{:S(2)}, u32[]{:S(2)}) collective-permute-start(s32[1,6]{1,0:T(1,128)S(1)} %add_bitcast_fusion), channel_id=1, source_target_pairs={{0,6},{2,0},{4,2},{6,4},{1,7},{3,1},{5,3},{7,5},{8,14},{10,8},{12,... | collective-permute-start | bytes 80 | tf_op jit(solution)/shard_map/ppermute | solution.py:31
  107.0 43.2 %collective-permute-start.15 = (bf16[1024,512]{1,0:T(8,128)(2,1)}, bf16[1024,512]{1,0:T(8,128)(2,1)}, u32[]{:S(2)}, u32[]{:S(2)}) collective-permute-start(bf16[1024,512]{1,0:T(8,128)(2,1)} %constant_dynamic-update-slice_fusion.7.refs_0_), channel_id=1, source_target_pairs={{0,64},{8,72},{16,80},{24,88},{32,96},{40,104},{48,112},{56,120},{... | collective-permute-start | bytes 3145736 | tf_op jit(solution)/shard_map/ppermute | solution.py:27
  110.0 41.4 %collective-permute-start.16 = (bf16[1024,512]{1,0:T(8,128)(2,1)}, bf16[1024,512]{1,0:T(8,128)(2,1)}, u32[]{:S(2)}, u32[]{:S(2)}) collective-permute-start(bf16[1024,512]{1,0:T(8,128)(2,1)} %constant_dynamic-update-slice_fusion.7.refs_0_), channel_id=1, source_target_pairs={{0,192},{8,200},{16,208},{24,216},{32,224},{40,232},{48,240},{56,2... | collective-permute-start | bytes 3145736 | tf_op jit(solution)/shard_map/ppermute | solution.py:27
  113.3 37.9 %copy-start.12 = (bf16[512,512]{1,0:T(8,128)(2,1)}, bf16[512,512]{1,0:T(8,128)(2,1)S(1)}, u32[]{:S(2)}) copy-start(bf16[512,512]{1,0:T(8,128)(2,1)S(1)} %collective-permute-done.20.refs_4_) | copy-start | bytes 1572868
  113.3 12.6 %collective-permute-start.21 = (bf16[512,512]{1,0:T(8,128)(2,1)S(1)}, bf16[512,512]{1,0:T(8,128)(2,1)}, u32[]{:S(2)}, u32[]{:S(2)}) collective-permute-start(bf16[512,512]{1,0:T(8,128)(2,1)S(1)} %collective-permute-done.20.refs_4_), channel_id=1, source_target_pairs={{0,8},{8,16},{16,24},{24,32},{32,40},{40,48},{48,56},{56,0},{64,72... | collective-permute-start | bytes 1572872 | tf_op jit(solution)/shard_map/ppermute | solution.py:22
  113.4 12.6 %collective-permute-start.24 = (bf16[512,512]{1,0:T(8,128)(2,1)}, bf16[512,512]{1,0:T(8,128)(2,1)}, u32[]{:S(2)}, u32[]{:S(2)}) collective-permute-start(bf16[512,512]{1,0:T(8,128)(2,1)} %collective-permute-done.23.refs_7_), channel_id=1, source_target_pairs={{0,56},{8,0},{16,8},{24,16},{32,24},{40,32},{48,40},{56,48},{64,12... | collective-permute-start | bytes 1572872 | tf_op jit(solution)/shard_map/ppermute | solution.py:22
  125.9 29.9 %collective-permute-start.22 = (bf16[512,512]{1,0:T(8,128)(2,1)}, bf16[512,512]{1,0:T(8,128)(2,1)S(1)}, u32[]{:S(2)}, u32[]{:S(2)}) collective-permute-start(bf16[512,512]{1,0:T(8,128)(2,1)} %collective-permute-done.21.refs_5_), channel_id=1, source_target_pairs={{0,8},{8,16},{16,24},{24,32},{32,40},{40,48},{48,56},{56,0},{64,72... | collective-permute-start | bytes 1572872 | tf_op jit(solution)/shard_map/ppermute | solution.py:22
  125.9 30.2 %collective-permute-start.25 = (bf16[512,512]{1,0:T(8,128)(2,1)}, bf16[512,512]{1,0:T(8,128)(2,1)S(1)}, u32[]{:S(2)}, u32[]{:S(2)}) collective-permute-start(bf16[512,512]{1,0:T(8,128)(2,1)} %collective-permute-done.24.refs_8_), channel_id=1, source_target_pairs={{0,56},{8,0},{16,8},{24,16},{32,24},{40,32},{48,40},{56,48},{64,12... | collective-permute-start | bytes 1572872 | tf_op jit(solution)/shard_map/ppermute | solution.py:22
  151.3 27.2 %collective-permute-start.26 = (bf16[512,512]{1,0:T(8,128)(2,1)S(1)}, bf16[512,512]{1,0:T(8,128)(2,1)S(1)}, u32[]{:S(2)}, u32[]{:S(2)}) collective-permute-start(bf16[512,512]{1,0:T(8,128)(2,1)S(1)} %slice.153), channel_id=1, source_target_pairs={{0,64},{8,72},{16,80},{24,88},{32,96},{40,104},{48,112},{56,120},{... | collective-permute-start | bytes 1572872 | tf_op jit(solution)/shard_map/ppermute | solution.py:27
  152.5 26.0 %collective-permute-start.27 = (bf16[512,512]{1,0:T(8,128)(2,1)S(1)}, bf16[512,512]{1,0:T(8,128)(2,1)S(1)}, u32[]{:S(2)}, u32[]{:S(2)}) collective-permute-start(bf16[512,512]{1,0:T(8,128)(2,1)S(1)} %slice.154), channel_id=1, source_target_pairs={{0,192},{8,200},{16,208},{24,216},{32,224},{40,232},{48,240},{56,2... | collective-permute-start | bytes 1572872 | tf_op jit(solution)/shard_map/ppermute | solution.py:27
  155.8 3.7 %copy-start.7 = (bf16[512,512]{1,0:T(8,128)(2,1)}, bf16[512,512]{1,0:T(8,128)(2,1)S(1)}, u32[]{:S(2)}) copy-start(bf16[512,512]{1,0:T(8,128)(2,1)S(1)} %collective-permute-done.22.refs_6_) | copy-start | bytes 1572868
  155.8 22.6 %collective-permute-start.28 = (bf16[256,512]{1,0:T(8,128)(2,1)S(1)}, bf16[256,512]{1,0:T(8,128)(2,1)S(1)}, u32[]{:S(2)}, u32[]{:S(2)}) collective-permute-start(bf16[256,512]{1,0:T(8,128)(2,1)S(1)} %slice.155), channel_id=1, source_target_pairs={{0,8},{8,16},{16,24},{24,32},{32,40},{40,48},{48,56},{56,0},{64,72... | collective-permute-start | bytes 786440 | tf_op jit(solution)/shard_map/ppermute | solution.py:22
  156.1 3.3 %copy-start.8 = (bf16[512,512]{1,0:T(8,128)(2,1)}, bf16[512,512]{1,0:T(8,128)(2,1)S(1)}, u32[]{:S(2)}) copy-start(bf16[512,512]{1,0:T(8,128)(2,1)S(1)} %collective-permute-done.25.refs_9_) | copy-start | bytes 1572868
  156.1 22.3 %collective-permute-start.29 = (bf16[256,512]{1,0:T(8,128)(2,1)S(1)}, bf16[256,512]{1,0:T(8,128)(2,1)S(1)}, u32[]{:S(2)}, u32[]{:S(2)}) collective-permute-start(bf16[256,512]{1,0:T(8,128)(2,1)S(1)} %slice.156), channel_id=1, source_target_pairs={{0,56},{8,0},{16,8},{24,16},{32,24},{40,32},{48,40},{56,48},{64,12... | collective-permute-start | bytes 786440 | tf_op jit(solution)/shard_map/ppermute | solution.py:22
  178.5 1.2 copy-start.14
  190.5 7.0 %collective-permute-start.30 = (bf16[8,80,128]{2,1,0:T(8,128)(2,1)}, bf16[8,80,128]{2,1,0:T(8,128)(2,1)S(1)}, u32[]{:S(2)}, u32[]{:S(2)}) collective-permute-start(bf16[8,80,128]{2,1,0:T(8,128)(2,1)} %shard_map.75.own), channel_id=1, source_target_pairs={{0,4},{2,6},{4,0},{6,2},{1,5},{3,7},{5,1},{7,3},{8,12},{10,14},{12... | collective-permute-start | bytes 491528 | tf_op jit(solution)/shard_map/ppermute | solution.py:31
  192.3 6.1 %collective-permute-start.31 = (bf16[8,80,128]{2,1,0:T(8,128)(2,1)}, bf16[8,80,128]{2,1,0:T(8,128)(2,1)S(1)}, u32[]{:S(2)}, u32[]{:S(2)}) collective-permute-start(bf16[8,80,128]{2,1,0:T(8,128)(2,1)} %shard_map.75.own), channel_id=1, source_target_pairs={{0,2},{2,4},{4,6},{6,0},{1,3},{3,5},{5,7},{7,1},{8,10},{10,12},{12... | collective-permute-start | bytes 491528 | tf_op jit(solution)/shard_map/ppermute | solution.py:31
  193.0 6.7 %collective-permute-start.32 = (bf16[8,80,128]{2,1,0:T(8,128)(2,1)}, bf16[8,80,128]{2,1,0:T(8,128)(2,1)S(1)}, u32[]{:S(2)}, u32[]{:S(2)}) collective-permute-start(bf16[8,80,128]{2,1,0:T(8,128)(2,1)} %shard_map.75.own), channel_id=1, source_target_pairs={{0,6},{2,0},{4,2},{6,4},{1,7},{3,1},{5,3},{7,5},{8,14},{10,8},{12,... | collective-permute-start | bytes 491528 | tf_op jit(solution)/shard_map/ppermute | solution.py:31
  197.6 2.2 %copy-start.3 = (bf16[8,80,128]{2,1,0:T(8,128)(2,1)}, bf16[8,80,128]{2,1,0:T(8,128)(2,1)S(1)}, u32[]{:S(2)}) copy-start(bf16[8,80,128]{2,1,0:T(8,128)(2,1)S(1)} %collective-permute-done.30.opposite) | copy-start | bytes 491524
  198.4 1.3 copy-start.4
  (4 other events, 3.1 us)
